TPU v7x, 32 devices: a whole 2x2x4 slice. The times are simulated.
32 devices in a mesh: groups: 2 (over x), space: 16 (over z, y, core).
Axes of the slice: x: 2, y: 2, z: 4, core: 2. Of those that a mesh axis runs over, the one named last changes fastest.
Arguments:
- node_latent: bfloat16 [12288, 512], P(('groups', 'space')), parts along dimension 0, may hold values from -6 to 6
- edge_latent: bfloat16 [65536, 512], P(('groups', 'space')), parts along dimension 0, may hold values from -6 to 6
- sender_local: int32 [32768], P('space'), may hold values from 0 to 383
- receiver_target: int32 [32768], P('space'), may hold values from 0 to 639, as said below
- row_list: int32 [16, 16, 16], P('space'), may hold values from 0 to 383
- edge_count: int32 [16], P('space'), may hold values from 1 to 2048, 16384 in all
- edge_in: bfloat16 [1536, 512], replicated, may hold values from -0.15625 to 0.15625
- edge_out: bfloat16 [512, 512], replicated, may hold values from -0.25 to 0.25
- node_in: bfloat16 [1024, 512], replicated, may hold values from -0.1875 to 0.1875
- node_out: bfloat16 [512, 512], replicated, may hold values from -0.25 to 0.25
Outputs:
- new_nodes: bfloat16 [12288, 512], P(('groups', 'space')), parts along dimension 0
- new_edges: bfloat16 [65536, 512], P(('groups', 'space')), parts along dimension 0
There are 2 independent parts, one for each index of `groups`. A program takes and returns all parts, laid end to end along the dimension named above; an argument that names none is the same for every part. Nothing has to cross between parts.
Inputs may be any that keep to these rules, and one draw needn't show every extreme that they name: `receiver_target`: an entry below 384 names a node of the slot's own device; an entry t of 384 or more names slot (t - 384) % 16 of device (t - 384) // 16, never the slot's own device.
All inputs are finite; a program needn't handle non-finite values. No bound on the sum of `edge_count` on one device may be relied on, other than what follows from the above.
Results may differ from a plain program's by a relative error of at most 0.0052.
Values may be sent and summed in bfloat16 or wider, within the bound.
A program may use at most 64 MiB of HBM per device.

v0:
```python
import jax
import jax.numpy as jnp
from jax import lax
from jax.sharding import PartitionSpec as P

epsilon = 1e-05


def normalize(values):
    center = values - jnp.mean(values, axis=-1, keepdims=True)
    spread = jnp.mean(center * center, axis=-1, keepdims=True)
    return center * lax.rsqrt(spread + epsilon)


def finish_update(latent, first, second_weight):
    hidden = jax.nn.silu(first).astype(jnp.bfloat16)
    mixed_out = jnp.dot(hidden, second_weight, preferred_element_type=jnp.float32)
    return (latent.astype(jnp.float32) + normalize(mixed_out)).astype(jnp.bfloat16)


def one_hot_rows(index, count, dtype):
    return (index[:, None] == jnp.arange(count, dtype=jnp.int32)[None, :]).astype(dtype)


def pick_half(index, table):
    return jnp.dot(
        one_hot_rows(index, table.shape[0], jnp.bfloat16), table, preferred_element_type=jnp.float32
    ).astype(jnp.bfloat16)


def spread_half(index, count, values):
    return lax.dot_general(
        one_hot_rows(index, count, jnp.bfloat16),
        values,
        (((0,), (0,)), ((), ())),
        preferred_element_type=jnp.float32,
    )


def spread_full(index, count, values):
    return lax.dot_general(
        one_hot_rows(index, count, jnp.float32),
        values,
        (((0,), (0,)), ((), ())),
        preferred_element_type=jnp.float32,
        precision=lax.Precision.HIGHEST,
    )


def shards(
    node_latent,
    edge_latent,
    sender_local,
    receiver_target,
    row_list,
    edge_count,
    edge_in,
    edge_out,
    node_in,
    node_out,
):
    peer_total = lax.axis_size("space")
    node_dev, width = node_latent.shape
    edge_dev = edge_latent.shape[0]
    capacity = row_list.shape[2]
    slot_total = node_dev + peer_total * capacity
    wanted = row_list[0].reshape(peer_total * capacity)
    w_edge = edge_in[:width]
    w_send = edge_in[width : 2 * width]
    w_recv = edge_in[2 * width :]
    outgoing = pick_half(wanted, node_latent).reshape(peer_total, capacity, width)
    arrived = lax.all_to_all(outgoing, "space", split_axis=0, concat_axis=0, tiled=True)
    row_table = jnp.concatenate(
        [node_latent, arrived.reshape(peer_total * capacity, width)], axis=0
    )

    def first_layer(edge_rows, send_index, recv_index):
        total = jnp.dot(edge_rows, w_edge, preferred_element_type=jnp.float32)
        total = total + jnp.dot(
            pick_half(send_index, node_latent), w_send, preferred_element_type=jnp.float32
        )
        return total + jnp.dot(
            pick_half(recv_index, row_table), w_recv, preferred_element_type=jnp.float32
        )

    live_count = edge_count[0]

    def update_rows(edge_rows, send_index, recv_index, row_ids):
        updated = finish_update(edge_rows, first_layer(edge_rows, send_index, recv_index), edge_out)
        live_rows = row_ids < live_count
        kept_rows = jnp.where(live_rows[:, None], updated, edge_rows)
        messages = jnp.where(live_rows[:, None], updated, jnp.zeros((), jnp.bfloat16))
        return (kept_rows, spread_half(recv_index, slot_total, messages))

    block_rows = 512
    block_total = edge_dev // block_rows

    def one_step(slot_sums, pieces):
        edge_rows, send_index, recv_index, row_ids = pieces
        kept_rows, block_sums = update_rows(edge_rows, send_index, recv_index, row_ids)
        return (slot_sums + block_sums, kept_rows)

    pieces = (
        edge_latent.reshape(block_total, block_rows, width),
        sender_local.reshape(block_total, block_rows),
        receiver_target.reshape(block_total, block_rows),
        jnp.arange(edge_dev, dtype=jnp.int32).reshape(block_total, block_rows),
    )
    slot_sums, kept_blocks = lax.scan(one_step, jnp.zeros((slot_total, width), jnp.float32), pieces)
    new_edges = kept_blocks.reshape(edge_dev, width)
    remote_sums = slot_sums[node_dev:].reshape(peer_total, capacity, width)
    returned = lax.all_to_all(remote_sums, "space", split_axis=0, concat_axis=0, tiled=True)
    aggregate = slot_sums[:node_dev] + spread_full(
        wanted, node_dev, returned.reshape(peer_total * capacity, width)
    )
    node_first = jnp.dot(node_latent, node_in[:width], preferred_element_type=jnp.float32)
    node_first = node_first + jnp.dot(
        aggregate.astype(jnp.bfloat16), node_in[width:], preferred_element_type=jnp.float32
    )
    new_nodes = finish_update(node_latent, node_first, node_out)
    return (new_nodes, new_edges)


def solution(mesh):
    in_specs = (
        P(("groups", "space"), None),
        P(("groups", "space"), None),
        P("space"),
        P("space"),
        P("space", None, None),
        P("space"),
        P(),
        P(),
        P(),
        P(),
    )
    out_specs = (P(("groups", "space"), None), P(("groups", "space"), None))
    return jax.shard_map(shards, mesh=mesh, in_specs=in_specs, out_specs=out_specs, check_vma=False)
```

profile of v0, /device:TPU:0, one launch (start us, length us, event | category | flops | bytes accessed | tf_op | source)
XLA Modules:
  0.0 100.2 jit_solution(10736769540244323018)
XLA Ops:
  0.6 0.8 eq.24
  1.5 2.1 %convolution_convert_fusion.1 = bf16[256,512]{1,0:T(8,128)(2,1)} fusion(bf16[384,512]{1,0:T(8,128)(2,1)} %param.12, s32[256]{0:T(256)S(1)} %eq.24), kind=kOutput, calls=%fused_computation.33 | convolution fusion | flops 100892672 | bytes 656384 | tf_op jit(solution)/shard_map/dot_general | solution.py:26
  3.5 7.4 %all-to-all-start = ((bf16[16,16,512]{2,1,0:T(8,128)(2,1)}), bf16[16,16,512]{2,1,0:T(8,128)(2,1)S(1)}, u32[]{:S(2)}, u32[]{:S(2)}) async-start(bf16[16,16,512]{2,1,0:T(8,128)(2,1)} %bitcast.2), calls=%async_computation | async-start | bytes 524288 | tf_op jit(solution)/shard_map/all_to_all | solution.py:72
  10.9 0.7 reshape.71
  11.7 0.7 reshape.76
  12.4 2.5 %fusion.27 = (bf16[512,512]{1,0:T(8,128)(2,1)}, bf16[512,512]{1,0:T(8,128)(2,1)S(1)}, bf16[512,512]{1,0:T(8,128)(2,1)}) fusion(bf16[1536,512]{1,0:T(8,128)(2,1)} %param.18), kind=kLoop, calls=%fused_computation.51 | loop fusion | bytes 3145728 | tf_op jit(solution)/shard_map/slice | solution.py:70
  14.9 6.1 %all-to-all-done = bf16[16,16,512]{2,1,0:T(8,128)(2,1)S(1)} async-done(((bf16[16,16,512]{2,1,0:T(8,128)(2,1)}), bf16[16,16,512]{2,1,0:T(8,128)(2,1)S(1)}, u32[]{:S(2)}, u32[]{:S(2)}) %all-to-all-start) | async-done | bytes 262176 | tf_op jit(solution)/shard_map/all_to_all | solution.py:72
  21.0 0.9 pad_maximum_fusion
  21.9 53.8 %while.13 = (s32[]{:T(128)}, f32[640,512]{1,0:T(8,128)}, bf16[4,512,512]{2,1,0:T(8,128)(2,1)}, s32[4,512]{1,0:T(4,128)S(1)}, s32[4,512]{1,0:T(4,128)S(1)}, /*ind...) while((s32[]{:T(128)}, f32[640,512]{1,0:T(8,128)}, ...), condition=%wide.region_3.4_spmd.clone, body=%wide.region_0.3_spmd.clone.sunk | while | flops 1954546688 | bytes 25927580 | solution.py:109
  21.9 0.7 compare_reduce_fusion.2
  22.6 1.1 %constant_dynamic-slice_fusion.6 = bf16[1,512,512]{2,1,0:T(8,128)(2,1)S(1)} fusion(bf16[4,512,512]{2,1,0:T(8,128)(2,1)} %get-tuple-element.304, s32[]{:T(128)S(6)} %copy.26), kind=kLoop, calls=%fused_computation.26.clone.1 | loop fusion | bytes 1048580 | tf_op jit(solution)/shard_map/while/body/jit(dynamic_index_in_dim)/dynamic_slice | solution.py:109
  23.7 0.4 fusion.66
  24.2 1.8 %convolution_add_fusion.7 = f32[512,512]{1,0:T(8,128)S(1)} fusion(f32[512,512]{1,0:T(8,128)S(1)} %fusion.66, bf16[512,512]{1,0:T(8,128)(2,1)} %get-tuple-element.308, bf16[384,512]{1,0:T(8,128)(2,1)S(1)} %get-tuple-element.307, s32[512]{0:T(512)S(1)} %bitcast.67), kind=kOutput, calls=%fused_computation.2.clone.1 | convolution fusion | flops 470482944 | bytes 3016704 | tf_op jit(solution)/shard_map/while/body/eval_jaxpr/dot_general | solution.py:79
  26.0 3.1 %multiply_convert_fusion.3 = bf16[512,512]{1,0:T(8,128)(2,1)} fusion(f32[512,512]{1,0:T(8,128)S(1)} %convolution_add_fusion.7, bf16[512,512]{1,0:T(8,128)(2,1)} %get-tuple-element.310, bf16[640,512]{1,0:T(8,128)(2,1)} %get-tuple-element.309, s32[512]{0:T(512)S(1)} %bitcast.65), kind=kOutput, calls=%fused_computation.10.clone.1 | convolution fusion | flops 606142464 | bytes 2754560 | tf_op jit(solution)/shard_map/while/body/eval_jaxpr/dot_general | solution.py:82
  29.1 1.7 %fusion.67 = (f32[512]{0:T(512)S(1)}, f32[512,512]{0,1:T(8,128)S(1)}) fusion(bf16[512,512]{1,0:T(8,128)(2,1)} %multiply_convert_fusion.3, bf16[512,512]{1,0:T(8,128)(2,1)} %get-tuple-element.311), kind=kOutput, calls=%fused_computation.50.clone.1 | convolution fusion | flops 268697088 | bytes 2099200 | tf_op jit(solution)/shard_map/while/body/eval_jaxpr/dot_general | solution.py:17
  30.8 0.2 copy.20
  31.0 0.2 multiply_reduce_fusion.3
  31.2 1.8 %convolution_add_fusion.8 = f32[640,512]{1,0:T(8,128)} fusion(f32[640,512]{1,0:T(8,128)} %get-tuple-element.283, s32[512]{0:T(512)S(1)} %bitcast.66, pred[]{:T(512)S(6)} %compare.3, pred[512]{0:T(512)(128)(4,1)S(1)} %compare_reduce_fusion.2, f32[512,512]{0,1:T(8,128)S(1)} %get-tuple-element.264, bf16[1,512,512]{1,2,0:T(8,128)(2,1)S(1)} %copy.20, ...), kind=kOutput, calls=%fused_computation.clone.1 | convolution fusion | flops 338427904 | bytes 4200961 | tf_op jit(solution)/shard_map/while/body/eval_jaxpr/dot_general | solution.py:32
  33.0 0.2 fusion.68
  33.2 0.2 copy.21
  33.5 0.8 constant_dynamic-update-slice_fusion.2
  34.4 0.7 compare_reduce_fusion.2
  35.1 1.1 %constant_dynamic-slice_fusion.6 = bf16[1,512,512]{2,1,0:T(8,128)(2,1)S(1)} fusion(bf16[4,512,512]{2,1,0:T(8,128)(2,1)} %get-tuple-element.304, s32[]{:T(128)S(6)} %copy.26), kind=kLoop, calls=%fused_computation.26.clone.1 | loop fusion | bytes 1048580 | tf_op jit(solution)/shard_map/while/body/jit(dynamic_index_in_dim)/dynamic_slice | solution.py:109
  36.2 0.4 fusion.66
  36.7 1.8 %convolution_add_fusion.7 = f32[512,512]{1,0:T(8,128)S(1)} fusion(f32[512,512]{1,0:T(8,128)S(1)} %fusion.66, bf16[512,512]{1,0:T(8,128)(2,1)} %get-tuple-element.308, bf16[384,512]{1,0:T(8,128)(2,1)S(1)} %get-tuple-element.307, s32[512]{0:T(512)S(1)} %bitcast.67), kind=kOutput, calls=%fused_computation.2.clone.1 | convolution fusion | flops 470482944 | bytes 3016704 | tf_op jit(solution)/shard_map/while/body/eval_jaxpr/dot_general | solution.py:79
  38.5 3.1 %multiply_convert_fusion.3 = bf16[512,512]{1,0:T(8,128)(2,1)} fusion(f32[512,512]{1,0:T(8,128)S(1)} %convolution_add_fusion.7, bf16[512,512]{1,0:T(8,128)(2,1)} %get-tuple-element.310, bf16[640,512]{1,0:T(8,128)(2,1)} %get-tuple-element.309, s32[512]{0:T(512)S(1)} %bitcast.65), kind=kOutput, calls=%fused_computation.10.clone.1 | convolution fusion | flops 606142464 | bytes 2754560 | tf_op jit(solution)/shard_map/while/body/eval_jaxpr/dot_general | solution.py:82
  41.6 1.7 %fusion.67 = (f32[512]{0:T(512)S(1)}, f32[512,512]{0,1:T(8,128)S(1)}) fusion(bf16[512,512]{1,0:T(8,128)(2,1)} %multiply_convert_fusion.3, bf16[512,512]{1,0:T(8,128)(2,1)} %get-tuple-element.311), kind=kOutput, calls=%fused_computation.50.clone.1 | convolution fusion | flops 268697088 | bytes 2099200 | tf_op jit(solution)/shard_map/while/body/eval_jaxpr/dot_general | solution.py:17
  43.3 0.2 copy.20
  43.5 0.2 multiply_reduce_fusion.3
  43.7 3.1 %convolution_add_fusion.8 = f32[640,512]{1,0:T(8,128)} fusion(f32[640,512]{1,0:T(8,128)} %get-tuple-element.283, s32[512]{0:T(512)S(1)} %bitcast.66, pred[]{:T(512)S(6)} %compare.3, pred[512]{0:T(512)(128)(4,1)S(1)} %compare_reduce_fusion.2, f32[512,512]{0,1:T(8,128)S(1)} %get-tuple-element.264, bf16[1,512,512]{1,2,0:T(8,128)(2,1)S(1)} %copy.20, ...), kind=kOutput, calls=%fused_computation.clone.1 | convolution fusion | flops 338427904 | bytes 4200961 | tf_op jit(solution)/shard_map/while/body/eval_jaxpr/dot_general | solution.py:32
  46.8 0.2 fusion.68
  47.0 0.2 copy.21
  47.2 0.8 constant_dynamic-update-slice_fusion.2
  48.2 0.7 compare_reduce_fusion.2
  48.9 1.1 %constant_dynamic-slice_fusion.6 = bf16[1,512,512]{2,1,0:T(8,128)(2,1)S(1)} fusion(bf16[4,512,512]{2,1,0:T(8,128)(2,1)} %get-tuple-element.304, s32[]{:T(128)S(6)} %copy.26), kind=kLoop, calls=%fused_computation.26.clone.1 | loop fusion | bytes 1048580 | tf_op jit(solution)/shard_map/while/body/jit(dynamic_index_in_dim)/dynamic_slice | solution.py:109
  50.0 0.4 fusion.66
  50.4 1.8 %convolution_add_fusion.7 = f32[512,512]{1,0:T(8,128)S(1)} fusion(f32[512,512]{1,0:T(8,128)S(1)} %fusion.66, bf16[512,512]{1,0:T(8,128)(2,1)} %get-tuple-element.308, bf16[384,512]{1,0:T(8,128)(2,1)S(1)} %get-tuple-element.307, s32[512]{0:T(512)S(1)} %bitcast.67), kind=kOutput, calls=%fused_computation.2.clone.1 | convolution fusion | flops 470482944 | bytes 3016704 | tf_op jit(solution)/shard_map/while/body/eval_jaxpr/dot_general | solution.py:79
  52.2 3.1 %multiply_convert_fusion.3 = bf16[512,512]{1,0:T(8,128)(2,1)} fusion(f32[512,512]{1,0:T(8,128)S(1)} %convolution_add_fusion.7, bf16[512,512]{1,0:T(8,128)(2,1)} %get-tuple-element.310, bf16[640,512]{1,0:T(8,128)(2,1)} %get-tuple-element.309, s32[512]{0:T(512)S(1)} %bitcast.65), kind=kOutput, calls=%fused_computation.10.clone.1 | convolution fusion | flops 606142464 | bytes 2754560 | tf_op jit(solution)/shard_map/while/body/eval_jaxpr/dot_general | solution.py:82
  55.3 1.7 %fusion.67 = (f32[512]{0:T(512)S(1)}, f32[512,512]{0,1:T(8,128)S(1)}) fusion(bf16[512,512]{1,0:T(8,128)(2,1)} %multiply_convert_fusion.3, bf16[512,512]{1,0:T(8,128)(2,1)} %get-tuple-element.311), kind=kOutput, calls=%fused_computation.50.clone.1 | convolution fusion | flops 268697088 | bytes 2099200 | tf_op jit(solution)/shard_map/while/body/eval_jaxpr/dot_general | solution.py:17
  57.0 0.2 copy.20
  57.3 0.2 multiply_reduce_fusion.3
  57.4 3.1 %convolution_add_fusion.8 = f32[640,512]{1,0:T(8,128)} fusion(f32[640,512]{1,0:T(8,128)} %get-tuple-element.283, s32[512]{0:T(512)S(1)} %bitcast.66, pred[]{:T(512)S(6)} %compare.3, pred[512]{0:T(512)(128)(4,1)S(1)} %compare_reduce_fusion.2, f32[512,512]{0,1:T(8,128)S(1)} %get-tuple-element.264, bf16[1,512,512]{1,2,0:T(8,128)(2,1)S(1)} %copy.20, ...), kind=kOutput, calls=%fused_computation.clone.1 | convolution fusion | flops 338427904 | bytes 4200961 | tf_op jit(solution)/shard_map/while/body/eval_jaxpr/dot_general | solution.py:32
  60.6 0.2 fusion.68
  60.8 0.2 copy.21
  61.0 0.8 constant_dynamic-update-slice_fusion.2
  62.0 0.7 compare_reduce_fusion.2
  62.7 1.1 %constant_dynamic-slice_fusion.6 = bf16[1,512,512]{2,1,0:T(8,128)(2,1)S(1)} fusion(bf16[4,512,512]{2,1,0:T(8,128)(2,1)} %get-tuple-element.304, s32[]{:T(128)S(6)} %copy.26), kind=kLoop, calls=%fused_computation.26.clone.1 | loop fusion | bytes 1048580 | tf_op jit(solution)/shard_map/while/body/jit(dynamic_index_in_dim)/dynamic_slice | solution.py:109
  63.8 0.4 fusion.66
  64.2 1.8 %convolution_add_fusion.7 = f32[512,512]{1,0:T(8,128)S(1)} fusion(f32[512,512]{1,0:T(8,128)S(1)} %fusion.66, bf16[512,512]{1,0:T(8,128)(2,1)} %get-tuple-element.308, bf16[384,512]{1,0:T(8,128)(2,1)S(1)} %get-tuple-element.307, s32[512]{0:T(512)S(1)} %bitcast.67), kind=kOutput, calls=%fused_computation.2.clone.1 | convolution fusion | flops 470482944 | bytes 3016704 | tf_op jit(solution)/shard_map/while/body/eval_jaxpr/dot_general | solution.py:79
  66.0 3.1 %multiply_convert_fusion.3 = bf16[512,512]{1,0:T(8,128)(2,1)} fusion(f32[512,512]{1,0:T(8,128)S(1)} %convolution_add_fusion.7, bf16[512,512]{1,0:T(8,128)(2,1)} %get-tuple-element.310, bf16[640,512]{1,0:T(8,128)(2,1)} %get-tuple-element.309, s32[512]{0:T(512)S(1)} %bitcast.65), kind=kOutput, calls=%fused_computation.10.clone.1 | convolution fusion | flops 606142464 | bytes 2754560 | tf_op jit(solution)/shard_map/while/body/eval_jaxpr/dot_general | solution.py:82
  69.1 1.7 %fusion.67 = (f32[512]{0:T(512)S(1)}, f32[512,512]{0,1:T(8,128)S(1)}) fusion(bf16[512,512]{1,0:T(8,128)(2,1)} %multiply_convert_fusion.3, bf16[512,512]{1,0:T(8,128)(2,1)} %get-tuple-element.311), kind=kOutput, calls=%fused_computation.50.clone.1 | convolution fusion | flops 268697088 | bytes 2099200 | tf_op jit(solution)/shard_map/while/body/eval_jaxpr/dot_general | solution.py:17
  70.8 0.2 copy.20
  71.2 3.1 %convolution_add_fusion.8 = f32[640,512]{1,0:T(8,128)} fusion(f32[640,512]{1,0:T(8,128)} %get-tuple-element.283, s32[512]{0:T(512)S(1)} %bitcast.66, pred[]{:T(512)S(6)} %compare.3, pred[512]{0:T(512)(128)(4,1)S(1)} %compare_reduce_fusion.2, f32[512,512]{0,1:T(8,128)S(1)} %get-tuple-element.264, bf16[1,512,512]{1,2,0:T(8,128)(2,1)S(1)} %copy.20, ...), kind=kOutput, calls=%fused_computation.clone.1 | convolution fusion | flops 338427904 | bytes 4200961 | tf_op jit(solution)/shard_map/while/body/eval_jaxpr/dot_general | solution.py:32
  74.3 0.2 fusion.68
  74.6 0.2 copy.21
  74.8 0.8 constant_dynamic-update-slice_fusion.2
  75.7 1.9 %slice.26 = f32[256,512]{1,0:T(8,128)} slice(f32[640,512]{1,0:T(8,128)} %get-tuple-element.75), slice={[384:640], [0:512]} | slice | bytes 1048576 | tf_op jit(solution)/shard_map/slice | solution.py:111
  77.5 3.7 %all-to-all-start.1 = ((f32[16,16,512]{2,1,0:T(8,128)}), f32[16,16,512]{2,1,0:T(8,128)S(1)}, u32[]{:S(2)}, u32[]{:S(2)}) async-start(f32[16,16,512]{2,1,0:T(8,128)} %bitcast.4), calls=%async_computation.1 | async-start | bytes 1048576 | tf_op jit(solution)/shard_map/all_to_all | solution.py:112
  81.3 1.4 %fusion.20 = f32[384,512]{1,0:T(8,128)S(1)} fusion(bf16[384,512]{1,0:T(8,128)(2,1)S(1)} %get-tuple-element.314, bf16[1024,512]{1,0:T(8,128)(2,1)} %param.20), kind=kOutput, calls=%fused_computation.40 | convolution fusion | flops 201326592 | bytes 1703936 | tf_op jit(solution)/shard_map/dot_general | solution.py:116
  82.7 13.0 %all-to-all-done.1 = f32[16,16,512]{2,1,0:T(8,128)S(1)} async-done(((f32[16,16,512]{2,1,0:T(8,128)}), f32[16,16,512]{2,1,0:T(8,128)S(1)}, u32[]{:S(2)}, u32[]{:S(2)}) %all-to-all-start.1) | async-done | bytes 524320 | tf_op jit(solution)/shard_map/all_to_all | solution.py:112
  95.7 1.4 %fusion.16 = bf16[384,512]{1,0:T(8,128)(2,1)} fusion(f32[256,512]{1,0:T(8,128)S(1)} %bitcast.63, f32[640,512]{1,0:T(8,128)S(1)} %copy-done.1, s32[256]{0:T(256)S(1)} %eq.24), kind=kOutput, calls=%fused_computation.32 | convolution fusion | flops 604471296 | bytes 1704960 | tf_op jit(solution)/shard_map/dot_general | solution.py:41
  97.0 2.0 %fusion.28 = (f32[384]{0:T(512)S(1)}, f32[384,512]{1,0:T(8,128)S(1)}) fusion(bf16[512,512]{1,0:T(8,128)(2,1)S(1)} %copy-done, f32[384,512]{1,0:T(8,128)S(1)} %fusion.20, bf16[384,512]{1,0:T(8,128)(2,1)} %fusion.16, bf16[1024,512]{1,0:T(8,128)(2,1)} %param.20), kind=kOutput, calls=%fused_computation.52 | convolution fusion | flops 404029056 | bytes 3016192 | tf_op jit(solution)/shard_map/dot_general | solution.py:17
  99.0 0.2 multiply_reduce_fusion.1
  99.3 1.0 add_convert_fusion.2
  (88 shorter events, 0.5 us)
Async XLA Ops:
  0.6 96.4 %copy-start = (bf16[512,512]{1,0:T(8,128)(2,1)S(1)}, bf16[512,512]{1,0:T(8,128)(2,1)}, u32[]{:S(2)}) copy-start(bf16[512,512]{1,0:T(8,128)(2,1)} %param.21) | copy-start | bytes 1572868
  3.5 17.4 %all-to-all-start = ((bf16[16,16,512]{2,1,0:T(8,128)(2,1)}), bf16[16,16,512]{2,1,0:T(8,128)(2,1)S(1)}, u32[]{:S(2)}, u32[]{:S(2)}) async-start(bf16[16,16,512]{2,1,0:T(8,128)(2,1)} %bitcast.2), calls=%async_computation | async-start | bytes 524288 | tf_op jit(solution)/shard_map/all_to_all | solution.py:72
  12.4 8.6 %copy-start.2 = (bf16[384,512]{1,0:T(8,128)(2,1)S(1)}, bf16[384,512]{1,0:T(8,128)(2,1)}, u32[]{:S(2)}) copy-start(bf16[384,512]{1,0:T(8,128)(2,1)} %param.12) | copy-start | bytes 1179652
  21.9 2.3 %copy-start.3 = (bf16[512,512]{1,0:T(8,128)(2,1)}, bf16[512,512]{1,0:T(8,128)(2,1)S(1)}, u32[]{:S(2)}) copy-start(bf16[512,512]{1,0:T(8,128)(2,1)S(1)} %get-tuple-element.305) | copy-start | bytes 1572868 | tf_op jit(solution)/shard_map/while
  21.9 2.3 %copy-start.5 = (s32[4,512]{1,0:T(4,128)}, s32[4,512]{1,0:T(4,128)S(1)}, u32[]{:S(2)}) copy-start(s32[4,512]{1,0:T(4,128)S(1)} %get-tuple-element.301) | copy-start | bytes 24580 | tf_op jit(solution)/shard_map/while
  21.9 2.3 %copy-start.7 = (s32[4,512]{1,0:T(4,128)}, s32[4,512]{1,0:T(4,128)S(1)}, u32[]{:S(2)}) copy-start(s32[4,512]{1,0:T(4,128)S(1)} %get-tuple-element.306) | copy-start | bytes 24580 | tf_op jit(solution)/shard_map/while
  21.9 2.3 %copy-start.9 = (s32[4,512]{1,0:T(4,128)}, s32[4,512]{1,0:T(4,128)S(1)}, u32[]{:S(2)}) copy-start(s32[4,512]{1,0:T(4,128)S(1)} %get-tuple-element.302) | copy-start | bytes 24580 | tf_op jit(solution)/shard_map/while
  33.2 1.1 %copy-start.4 = (bf16[512,512]{1,0:T(8,128)(2,1)S(1)}, bf16[512,512]{1,0:T(8,128)(2,1)}, u32[]{:S(2)}) copy-start(bf16[512,512]{1,0:T(8,128)(2,1)} %copy-done.3) | copy-start | bytes 1572868 | tf_op jit(solution)/shard_map/while
  33.2 1.1 %copy-start.6 = (s32[4,512]{1,0:T(4,128)S(1)}, s32[4,512]{1,0:T(4,128)}, u32[]{:S(2)}) copy-start(s32[4,512]{1,0:T(4,128)} %copy-done.5) | copy-start | bytes 24580 | tf_op jit(solution)/shard_map/while
  33.2 1.1 %copy-start.8 = (s32[4,512]{1,0:T(4,128)S(1)}, s32[4,512]{1,0:T(4,128)}, u32[]{:S(2)}) copy-start(s32[4,512]{1,0:T(4,128)} %copy-done.7) | copy-start | bytes 24580 | tf_op jit(solution)/shard_map/while
  33.2 1.1 %copy-start.10 = (s32[4,512]{1,0:T(4,128)S(1)}, s32[4,512]{1,0:T(4,128)}, u32[]{:S(2)}) copy-start(s32[4,512]{1,0:T(4,128)} %copy-done.9) | copy-start | bytes 24580 | tf_op jit(solution)/shard_map/while
  34.3 2.3 %copy-start.3 = (bf16[512,512]{1,0:T(8,128)(2,1)}, bf16[512,512]{1,0:T(8,128)(2,1)S(1)}, u32[]{:S(2)}) copy-start(bf16[512,512]{1,0:T(8,128)(2,1)S(1)} %get-tuple-element.305) | copy-start | bytes 1572868 | tf_op jit(solution)/shard_map/while
  34.3 2.3 %copy-start.5 = (s32[4,512]{1,0:T(4,128)}, s32[4,512]{1,0:T(4,128)S(1)}, u32[]{:S(2)}) copy-start(s32[4,512]{1,0:T(4,128)S(1)} %get-tuple-element.301) | copy-start | bytes 24580 | tf_op jit(solution)/shard_map/while
  34.3 2.3 %copy-start.7 = (s32[4,512]{1,0:T(4,128)}, s32[4,512]{1,0:T(4,128)S(1)}, u32[]{:S(2)}) copy-start(s32[4,512]{1,0:T(4,128)S(1)} %get-tuple-element.306) | copy-start | bytes 24580 | tf_op jit(solution)/shard_map/while
  34.4 2.3 %copy-start.9 = (s32[4,512]{1,0:T(4,128)}, s32[4,512]{1,0:T(4,128)S(1)}, u32[]{:S(2)}) copy-start(s32[4,512]{1,0:T(4,128)S(1)} %get-tuple-element.302) | copy-start | bytes 24580 | tf_op jit(solution)/shard_map/while
  47.0 1.1 %copy-start.4 = (bf16[512,512]{1,0:T(8,128)(2,1)S(1)}, bf16[512,512]{1,0:T(8,128)(2,1)}, u32[]{:S(2)}) copy-start(bf16[512,512]{1,0:T(8,128)(2,1)} %copy-done.3) | copy-start | bytes 1572868 | tf_op jit(solution)/shard_map/while
  47.0 1.1 %copy-start.6 = (s32[4,512]{1,0:T(4,128)S(1)}, s32[4,512]{1,0:T(4,128)}, u32[]{:S(2)}) copy-start(s32[4,512]{1,0:T(4,128)} %copy-done.5) | copy-start | bytes 24580 | tf_op jit(solution)/shard_map/while
  47.0 1.1 %copy-start.8 = (s32[4,512]{1,0:T(4,128)S(1)}, s32[4,512]{1,0:T(4,128)}, u32[]{:S(2)}) copy-start(s32[4,512]{1,0:T(4,128)} %copy-done.7) | copy-start | bytes 24580 | tf_op jit(solution)/shard_map/while
  47.0 1.1 %copy-start.10 = (s32[4,512]{1,0:T(4,128)S(1)}, s32[4,512]{1,0:T(4,128)}, u32[]{:S(2)}) copy-start(s32[4,512]{1,0:T(4,128)} %copy-done.9) | copy-start | bytes 24580 | tf_op jit(solution)/shard_map/while
  48.1 2.3 %copy-start.3 = (bf16[512,512]{1,0:T(8,128)(2,1)}, bf16[512,512]{1,0:T(8,128)(2,1)S(1)}, u32[]{:S(2)}) copy-start(bf16[512,512]{1,0:T(8,128)(2,1)S(1)} %get-tuple-element.305) | copy-start | bytes 1572868 | tf_op jit(solution)/shard_map/while
  48.1 2.3 %copy-start.5 = (s32[4,512]{1,0:T(4,128)}, s32[4,512]{1,0:T(4,128)S(1)}, u32[]{:S(2)}) copy-start(s32[4,512]{1,0:T(4,128)S(1)} %get-tuple-element.301) | copy-start | bytes 24580 | tf_op jit(solution)/shard_map/while
  48.1 2.3 %copy-start.7 = (s32[4,512]{1,0:T(4,128)}, s32[4,512]{1,0:T(4,128)S(1)}, u32[]{:S(2)}) copy-start(s32[4,512]{1,0:T(4,128)S(1)} %get-tuple-element.306) | copy-start | bytes 24580 | tf_op jit(solution)/shard_map/while
  48.1 2.3 %copy-start.9 = (s32[4,512]{1,0:T(4,128)}, s32[4,512]{1,0:T(4,128)S(1)}, u32[]{:S(2)}) copy-start(s32[4,512]{1,0:T(4,128)S(1)} %get-tuple-element.302) | copy-start | bytes 24580 | tf_op jit(solution)/shard_map/while
  60.8 1.1 %copy-start.4 = (bf16[512,512]{1,0:T(8,128)(2,1)S(1)}, bf16[512,512]{1,0:T(8,128)(2,1)}, u32[]{:S(2)}) copy-start(bf16[512,512]{1,0:T(8,128)(2,1)} %copy-done.3) | copy-start | bytes 1572868 | tf_op jit(solution)/shard_map/while
  60.8 1.1 %copy-start.6 = (s32[4,512]{1,0:T(4,128)S(1)}, s32[4,512]{1,0:T(4,128)}, u32[]{:S(2)}) copy-start(s32[4,512]{1,0:T(4,128)} %copy-done.5) | copy-start | bytes 24580 | tf_op jit(solution)/shard_map/while
  60.8 1.1 %copy-start.8 = (s32[4,512]{1,0:T(4,128)S(1)}, s32[4,512]{1,0:T(4,128)}, u32[]{:S(2)}) copy-start(s32[4,512]{1,0:T(4,128)} %copy-done.7) | copy-start | bytes 24580 | tf_op jit(solution)/shard_map/while
  60.8 1.1 %copy-start.10 = (s32[4,512]{1,0:T(4,128)S(1)}, s32[4,512]{1,0:T(4,128)}, u32[]{:S(2)}) copy-start(s32[4,512]{1,0:T(4,128)} %copy-done.9) | copy-start | bytes 24580 | tf_op jit(solution)/shard_map/while
  61.9 2.3 %copy-start.3 = (bf16[512,512]{1,0:T(8,128)(2,1)}, bf16[512,512]{1,0:T(8,128)(2,1)S(1)}, u32[]{:S(2)}) copy-start(bf16[512,512]{1,0:T(8,128)(2,1)S(1)} %get-tuple-element.305) | copy-start | bytes 1572868 | tf_op jit(solution)/shard_map/while
  61.9 2.3 %copy-start.5 = (s32[4,512]{1,0:T(4,128)}, s32[4,512]{1,0:T(4,128)S(1)}, u32[]{:S(2)}) copy-start(s32[4,512]{1,0:T(4,128)S(1)} %get-tuple-element.301) | copy-start | bytes 24580 | tf_op jit(solution)/shard_map/while
  61.9 2.3 %copy-start.7 = (s32[4,512]{1,0:T(4,128)}, s32[4,512]{1,0:T(4,128)S(1)}, u32[]{:S(2)}) copy-start(s32[4,512]{1,0:T(4,128)S(1)} %get-tuple-element.306) | copy-start | bytes 24580 | tf_op jit(solution)/shard_map/while
  61.9 2.3 %copy-start.9 = (s32[4,512]{1,0:T(4,128)}, s32[4,512]{1,0:T(4,128)S(1)}, u32[]{:S(2)}) copy-start(s32[4,512]{1,0:T(4,128)S(1)} %get-tuple-element.302) | copy-start | bytes 24580 | tf_op jit(solution)/shard_map/while
  74.5 1.1 %copy-start.4 = (bf16[512,512]{1,0:T(8,128)(2,1)S(1)}, bf16[512,512]{1,0:T(8,128)(2,1)}, u32[]{:S(2)}) copy-start(bf16[512,512]{1,0:T(8,128)(2,1)} %copy-done.3) | copy-start | bytes 1572868 | tf_op jit(solution)/shard_map/while
  74.6 1.1 %copy-start.6 = (s32[4,512]{1,0:T(4,128)S(1)}, s32[4,512]{1,0:T(4,128)}, u32[]{:S(2)}) copy-start(s32[4,512]{1,0:T(4,128)} %copy-done.5) | copy-start | bytes 24580 | tf_op jit(solution)/shard_map/while
  74.6 1.1 %copy-start.8 = (s32[4,512]{1,0:T(4,128)S(1)}, s32[4,512]{1,0:T(4,128)}, u32[]{:S(2)}) copy-start(s32[4,512]{1,0:T(4,128)} %copy-done.7) | copy-start | bytes 24580 | tf_op jit(solution)/shard_map/while
  74.6 1.1 %copy-start.10 = (s32[4,512]{1,0:T(4,128)S(1)}, s32[4,512]{1,0:T(4,128)}, u32[]{:S(2)}) copy-start(s32[4,512]{1,0:T(4,128)} %copy-done.9) | copy-start | bytes 24580 | tf_op jit(solution)/shard_map/while
  77.5 18.1 %copy-start.1 = (f32[640,512]{1,0:T(8,128)S(1)}, f32[640,512]{1,0:T(8,128)}, u32[]{:S(2)}) copy-start(f32[640,512]{1,0:T(8,128)} %get-tuple-element.75) | copy-start | bytes 3932164
  77.5 18.1 %all-to-all-start.1 = ((f32[16,16,512]{2,1,0:T(8,128)}), f32[16,16,512]{2,1,0:T(8,128)S(1)}, u32[]{:S(2)}, u32[]{:S(2)}) async-start(f32[16,16,512]{2,1,0:T(8,128)} %bitcast.4), calls=%async_computation.1 | async-start | bytes 1048576 | tf_op jit(solution)/shard_map/all_to_all | solution.py:112
where the time goes:
time: 102 us; the launch traced here: 100 us
  matrix products  45.9 us (45%)
  waiting for transfers between devices  19.1 us (19%)
  local copies, waits for them, and re-layouts  16.2 us (16%)
  starting transfers between devices  11.1 us (11%)
  other arithmetic  6.58 us (6%)
    all_to_all x1, waiting for transfers between devices, shards(): lax.all_to_all(remote_sums, 'space', split_axis=0, concat_axis=0, tiled=T...  13 us
    dot_general x4, matrix products, first_layer(): jnp.dot(pick_half(recv_index, row_table), w_recv, preferred_element_type=...  12.4 us
    dot_general x4, matrix products, spread_half(): lax.dot_general(one_hot_rows(index, count, jnp.bfloat16), values, (((0,),...  11.1 us
    dot_general x5, matrix products, finish_update(): jnp.dot(hidden, second_weight, preferred_element_type=jnp.float32)  8.75 us
    all_to_all x1, starting transfers between devices, shards(): lax.all_to_all(outgoing, 'space', split_axis=0, concat_axis=0, tiled=True)  7.39 us
    dot_general x4, matrix products, first_layer(): jnp.dot(pick_half(send_index, node_latent), w_send, preferred_element_typ...  7.17 us
    all_to_all x1, waiting for transfers between devices, shards(): lax.all_to_all(outgoing, 'space', split_axis=0, concat_axis=0, tiled=True)  6.08 us
    dynamic_slice x12, local copies, waits for them, and re-layouts, shards(): lax.scan(one_step, jnp.zeros((slot_total, width), jnp.float32), pieces)  5.2 us
  transfers between devices with their start and end apart: 2, of which 2 were waited for; matrix products, arithmetic and copies ran while one was open for 5% of the time, Pallas kernels for 0%

commit v1 on v0

v1 whole, which is shorter than its diff:
```python
import functools

import jax
import jax.numpy as jnp
from jax import lax
from jax.experimental import pallas as pl
from jax.experimental.pallas import tpu as pltpu
from jax.sharding import PartitionSpec as P

epsilon = 1e-05
lanes = 128
block_rows = 256
MESH = pl.DeviceIdType.MESH
bf16 = jnp.bfloat16
f32 = jnp.float32


def dot(left, right):
    return jnp.dot(left, right, preferred_element_type=f32)


def iota(shape, axis):
    return lax.broadcasted_iota(jnp.int32, shape, axis)


def half_silu(first):
    half = 0.5 * first
    return (half + half * jnp.tanh(half)).astype(bf16)


def residual_norm(latent, mixed):
    center = mixed - jnp.mean(mixed, axis=-1, keepdims=True)
    spread = jnp.mean(center * center, axis=-1, keepdims=True)
    return latent.astype(f32) + center * lax.rsqrt(spread + epsilon)


def kernel(
    peers,
    pad,
    count_ref,
    node_hbm,
    edge_hbm,
    send_hbm,
    recv_hbm,
    list_hbm,
    edge_in_hbm,
    edge_out_hbm,
    node_in_hbm,
    node_out_hbm,
    new_nodes_hbm,
    new_edges_hbm,
    node_v,
    edge_v,
    send_v,
    recv_v,
    list_v,
    table_v,
    ends_v,
    edge_out_v,
    node_in_v,
    node_out_v,
    first_v,
    far_hot_v,
    spread_v,
    back_v,
    new_nodes_v,
    new_edges_v,
    out_rows,
    in_rows,
    out_sums,
    in_sums,
    load_sem,
    store_sem,
    sems,
):
    node_dev, width = node_v.shape
    edge_dev = edge_v.shape[0]
    slots = peers * pad
    near = width + 2 * node_dev
    blocks = edge_dev // block_rows
    parts = block_rows // lanes
    me = lax.axis_index("space")

    barrier = pltpu.get_barrier_semaphore()

    def greet(k, carry):
        peer = lax.rem(me + k, peers)
        pl.semaphore_signal(barrier, inc=1, device_id={"space": peer}, device_id_type=MESH)
        return carry

    lax.fori_loop(1, peers, greet, 0)

    loads = [
        pltpu.make_async_copy(source, target, load_sem.at[number])
        for number, (source, target) in enumerate(
            [
                (list_hbm, list_v),
                (node_hbm, node_v),
                (edge_in_hbm.at[pl.ds(width, 2 * width)], ends_v),
                (send_hbm, send_v),
                (recv_hbm, recv_v),
                (edge_in_hbm.at[pl.ds(0, width)], table_v.at[pl.ds(0, width)]),
                (edge_hbm, edge_v),
                (edge_out_hbm, edge_out_v),
                (node_in_hbm, node_in_v),
                (node_out_hbm, node_out_v),
            ]
        )
    ]
    for load in loads:
        load.start()

    own = pl.ds(pl.multiple_of(me * pad, pad), pad)
    in_rows[own, :] = jnp.zeros((pad, width), bf16)
    in_sums[own, :] = jnp.zeros((pad, width), bf16)

    loads[0].wait()
    listed = list_v[...]
    rows = jnp.concatenate(
        [jnp.broadcast_to(listed[p : p + 1], (pad, pad)) for p in range(peers)], axis=0
    ).astype(f32)
    picked = lax.rem(iota((slots, pad), 0), pad) == iota((slots, pad), 1)
    column = jnp.sum(jnp.where(picked, rows, 0.0), axis=1, keepdims=True)
    wanted = (column.astype(jnp.int32) == iota((slots, node_dev), 1)).astype(f32)
    loads[1].wait()
    out_rows[...] = dot(wanted.astype(bf16), node_v[...]).astype(bf16)

    def transfer(source, target, number, peer):
        theirs = pl.ds(pl.multiple_of(peer * pad, pad), pad)
        return pltpu.make_async_remote_copy(
            src_ref=source.at[theirs],
            dst_ref=target.at[own],
            send_sem=sems.at[number, peer],
            recv_sem=sems.at[number + 1, me],
            device_id={"space": peer},
            device_id_type=MESH,
        )

    def arrival(source, target, number, peer):
        theirs = pl.ds(pl.multiple_of(peer * pad, pad), pad)
        return pltpu.make_async_remote_copy(
            src_ref=source.at[theirs],
            dst_ref=target.at[theirs],
            send_sem=sems.at[number, peer],
            recv_sem=sems.at[number + 1, peer],
            device_id={"space": peer},
            device_id_type=MESH,
        )

    def each_peer(action):
        def step(k, carry):
            action(lax.rem(me + k, peers))
            return carry

        lax.fori_loop(1, peers, step, 0)

    pl.semaphore_wait(barrier, peers - 1)
    each_peer(lambda peer: transfer(out_rows, in_rows, 0, peer).start())

    back_v[...] = wanted.T.astype(bf16)
    loads[2].wait()
    table_v[pl.ds(width, node_dev), :] = dot(node_v[...], ends_v[pl.ds(0, width), :]).astype(bf16)
    table_v[pl.ds(width + node_dev, node_dev), :] = dot(
        node_v[...], ends_v[pl.ds(width, width), :]
    ).astype(bf16)
    for load in loads[3:]:
        load.wait()
    live_count = count_ref[0]

    def columns_of(index_ref, block):
        return jnp.concatenate(
            [
                jnp.broadcast_to(index_ref[pl.ds(block * parts + j, 1), :], (lanes, lanes)).T
                for j in range(parts)
            ],
            axis=0,
        )

    lane_ids = iota((block_rows, lanes), 1)

    def hot(columns, low, high):
        return jnp.concatenate(
            [(columns == lane_ids + c).astype(f32).astype(bf16) for c in range(low, high, lanes)],
            axis=1,
        )

    def before(block, carry):
        here = pl.ds(pl.multiple_of(block * block_rows, block_rows), block_rows)
        senders = columns_of(send_v, block)
        receivers = columns_of(recv_v, block)
        left = jnp.concatenate(
            [edge_v[here, :], hot(senders, 0, node_dev), hot(receivers, 0, node_dev)], axis=1
        )
        first_v[here, :] = dot(left, table_v[pl.ds(0, near), :])
        far_hot_v[here, :] = hot(receivers, node_dev, node_dev + slots)
        for j in range(parts):
            place = block * block_rows + j * lanes
            live = place + iota((1, lanes), 1) < live_count
            target = jnp.where(live, recv_v[pl.ds(block * parts + j, 1), :], -1)
            spread = target == iota((node_dev + slots, lanes), 0)
            spread_v[:, pl.ds(pl.multiple_of(place, lanes), lanes)] = spread.astype(f32).astype(
                bf16
            )
        return carry

    lax.fori_loop(0, blocks, before, 0)

    each_peer(lambda peer: arrival(out_rows, in_rows, 0, peer).wait_recv())
    table_v[pl.ds(near, slots), :] = dot(in_rows[...], ends_v[pl.ds(width, width), :]).astype(bf16)

    def store(block):
        here = pl.ds(pl.multiple_of(block * block_rows, block_rows), block_rows)
        return pltpu.make_async_copy(
            new_edges_v.at[here], new_edges_hbm.at[here], store_sem.at[block]
        )

    def after(block, carry):
        here = pl.ds(pl.multiple_of(block * block_rows, block_rows), block_rows)
        first = first_v[here, :] + dot(far_hot_v[here, :], table_v[pl.ds(near, slots), :])
        mixed = dot(half_silu(first), edge_out_v[...])
        old = edge_v[here, :]
        updated = residual_norm(old, mixed)
        live = block * block_rows + iota((block_rows, 1), 0) < live_count
        new_edges_v[here, :] = jnp.where(live, updated, old.astype(f32)).astype(bf16)
        store(block).start()
        return carry

    lax.fori_loop(0, blocks, after, 0)

    out_sums[...] = dot(spread_v[pl.ds(node_dev, slots), :], new_edges_v[...]).astype(bf16)
    each_peer(lambda peer: transfer(out_sums, in_sums, 2, peer).start())

    near_sums = dot(spread_v[pl.ds(0, node_dev), :], new_edges_v[...])
    node_first = dot(node_v[...], node_in_v[pl.ds(0, width), :])
    each_peer(lambda peer: arrival(out_sums, in_sums, 2, peer).wait_recv())
    aggregate = (near_sums + dot(back_v[...], in_sums[...])).astype(bf16)
    node_first = node_first + dot(aggregate, node_in_v[pl.ds(width, width), :])
    mixed = dot(half_silu(node_first), node_out_v[...])
    new_nodes_v[...] = residual_norm(node_v[...], mixed).astype(bf16)
    last = pltpu.make_async_copy(new_nodes_v, new_nodes_hbm, store_sem.at[blocks])
    last.start()
    each_peer(lambda peer: transfer(out_rows, in_rows, 0, peer).wait_send())
    each_peer(lambda peer: transfer(out_sums, in_sums, 2, peer).wait_send())

    def finish(block, carry):
        store(block).wait()
        return carry

    lax.fori_loop(0, blocks, finish, 0)
    last.wait()


def shards(
    node_latent,
    edge_latent,
    sender_local,
    receiver_target,
    row_list,
    edge_count,
    edge_in,
    edge_out,
    node_in,
    node_out,
):
    peers = lax.axis_size("space")
    node_dev, width = node_latent.shape
    edge_dev = edge_latent.shape[0]
    capacity = row_list.shape[2]
    pad = -(-capacity // 16) * 16
    listed = row_list.reshape(peers, capacity)
    if pad != capacity:
        listed = jnp.pad(listed, ((0, 0), (0, pad - capacity)), constant_values=-1)
        slot = receiver_target - node_dev
        receiver_target = jnp.where(
            slot < 0, receiver_target, node_dev + slot // capacity * pad + slot % capacity
        )
    slots = peers * pad
    blocks = edge_dev // block_rows
    any_space = pl.BlockSpec(memory_space=pl.ANY)
    index_shape = (edge_dev // lanes, lanes)
    return pl.pallas_call(
        functools.partial(kernel, peers, pad),
        out_shape=(
            jax.ShapeDtypeStruct(node_latent.shape, bf16),
            jax.ShapeDtypeStruct(edge_latent.shape, bf16),
        ),
        in_specs=[pl.BlockSpec(memory_space=pltpu.SMEM)] + [any_space] * 9,
        out_specs=(any_space, any_space),
        scratch_shapes=[
            pltpu.VMEM((node_dev, width), bf16),
            pltpu.VMEM((edge_dev, width), bf16),
            pltpu.VMEM(index_shape, jnp.int32),
            pltpu.VMEM(index_shape, jnp.int32),
            pltpu.VMEM((peers, pad), jnp.int32),
            pltpu.VMEM((width + 2 * node_dev + slots, width), bf16),
            pltpu.VMEM((2 * width, width), bf16),
            pltpu.VMEM((width, width), bf16),
            pltpu.VMEM((2 * width, width), bf16),
            pltpu.VMEM((width, width), bf16),
            pltpu.VMEM((edge_dev, width), f32),
            pltpu.VMEM((edge_dev, slots), bf16),
            pltpu.VMEM((node_dev + slots, edge_dev), bf16),
            pltpu.VMEM((node_dev, slots), bf16),
            pltpu.VMEM((node_dev, width), bf16),
            pltpu.VMEM((edge_dev, width), bf16),
            pltpu.VMEM((slots, width), bf16),
            pltpu.VMEM((slots, width), bf16),
            pltpu.VMEM((slots, width), bf16),
            pltpu.VMEM((slots, width), bf16),
            pltpu.SemaphoreType.DMA((10,)),
            pltpu.SemaphoreType.DMA((blocks + 1,)),
            pltpu.SemaphoreType.DMA((4, peers)),
        ],
        compiler_params=pltpu.CompilerParams(
            collective_id=0, has_side_effects=True, vmem_limit_bytes=56 * 1024 * 1024
        ),
    )(
        edge_count,
        node_latent,
        edge_latent,
        sender_local.reshape(index_shape),
        receiver_target.reshape(index_shape),
        listed,
        edge_in,
        edge_out,
        node_in,
        node_out,
    )


def solution(mesh):
    in_specs = (
        P(("groups", "space"), None),
        P(("groups", "space"), None),
        P("space"),
        P("space"),
        P("space", None, None),
        P("space"),
        P(),
        P(),
        P(),
        P(),
    )
    out_specs = (P(("groups", "space"), None), P(("groups", "space"), None))
    return jax.shard_map(shards, mesh=mesh, in_specs=in_specs, out_specs=out_specs, check_vma=False)
```

time: 102 us -> 34.4 us (0.34); the launches traced: 100 us -> 34.2 us
  matrix products: 45.9 us -> 0 us
  Pallas kernels: 0 us -> 28.1 us
  waiting for transfers between devices: 19.1 us -> 0 us
  local copies, waits for them, and re-layouts: 16.2 us -> 4.81 us
  starting transfers between devices: 11.1 us -> 0 us
  other arithmetic: 6.58 us -> 0 us
    dot_general x24 -> x0, matrix products: 45.9 us -> none  [the longest x4 12.4 us: first_layer(): jnp.dot(pick_half(recv_index, row_table), w_recv, preferred_element_type=...]
    pallas_call x0 -> x1, Pallas kernels: none -> 28.1 us  [shards(): pl.pallas_call(functools.partial(kernel, peers, pad), out_shape=(jax.Shap...]
    all_to_all x2 -> x0, waiting for transfers between devices: 19.1 us -> none  [the longest x1 13 us: shards(): lax.all_to_all(remote_sums, 'space', split_axis=0, concat_axis=0, tiled=T...]
    all_to_all x2 -> x0, starting transfers between devices: 11.1 us -> none  [the longest x1 7.39 us: shards(): lax.all_to_all(outgoing, 'space', split_axis=0, concat_axis=0, tiled=True)]
    dynamic_slice x12 -> x0, local copies, waits for them, and re-layouts: 5.2 us -> none  [shards(): lax.scan(one_step, jnp.zeros((slot_total, width), jnp.float32), pieces)]
    unnamed x6 -> x2, local copies, waits for them, and re-layouts: 0.02 us -> 4.81 us
    slice x2 -> x0, local copies, waits for them, and re-layouts: 4.41 us -> none  [the longest x1 2.53 us: shards(): w_recv = edge_in[2 * width:]]
    dynamic_update_slice x8 -> x0, local copies, waits for them, and re-layouts: 4.18 us -> none  [shards(): lax.scan(one_step, jnp.zeros((slot_total, width), jnp.float32), pieces)]
  transfers between devices with their start and end apart: 2 -> 0, of which waited for: 2 -> 0; matrix products, arithmetic and copies ran while one was open for 5% -> 0% of each run, Pallas kernels for 0% -> 0%
where the time goes in v1:
time: 34.4 us; the launch traced here: 34.2 us
  Pallas kernels  28.1 us (82%)
  local copies, waits for them, and re-layouts  4.81 us (14%)
  between operations  1.29 us (4%)
    pallas_call x1, Pallas kernels, shards(): pl.pallas_call(functools.partial(kernel, peers, pad), out_shape=(jax.Shap...  28.1 us
    unnamed x2, local copies, waits for them, and re-layouts  4.81 us

profile of v1, /device:TPU:0, one launch (start us, length us, event | category | flops | bytes accessed | tf_op | source)
XLA Modules:
  0.0 34.2 jit_solution(9189693305817538232)
XLA Ops:
  1.3 28.1 %shard_map.113 = (bf16[384,512]{1,0:T(8,128)(2,1)}, bf16[2048,512]{1,0:T(8,128)(2,1)}) custom-call(s32[1]{0:T(128)S(6)} %copy.14.count_ref, bf16[384,512]{1,0:T(8,128)(2,1)} %node_hbm.1, bf16[2048,512]{1,0:T(8,128)(2,1)} %edge_hbm.1, s32[16,128]{1,0:T(8,128)} %bitcast.3, s32[16,128]{1,0:T(8,128)} %bitcast.4, s32[16,16]{1,0:T(8,128)} %bitcast.5, ...), custom_call_target="tpu_custom_call" | custom-call | tf_op jit(solution)/shard_map/pallas_call | solution.py:281
  29.4 1.8 %copy.15 = bf16[384,512]{1,0:T(8,128)(2,1)} copy(bf16[384,512]{1,0:T(8,128)(2,1)} %get-tuple-element.4) | data formatting | bytes 786432
  31.2 3.0 %copy.16 = bf16[2048,512]{1,0:T(8,128)(2,1)} copy(bf16[2048,512]{1,0:T(8,128)(2,1)} %get-tuple-element.5) | data formatting | bytes 4194304

commit v2 on v1

--- a/solution.py
+++ b/solution.py
@@ -10,6 +10,7 @@
 epsilon = 1e-05
 lanes = 128
 block_rows = 256
+store_pieces = 4
 MESH = pl.DeviceIdType.MESH
 bf16 = jnp.bfloat16
 f32 = jnp.float32
@@ -47,9 +48,12 @@
     edge_out_hbm,
     node_in_hbm,
     node_out_hbm,
-    new_nodes_hbm,
-    new_edges_hbm,
+    new_edges_v,
+    aggregate_v,
+    node_first_v,
     node_v,
+    node_in_v,
+    node_out_v,
     edge_v,
     send_v,
     recv_v,
@@ -57,20 +61,16 @@
     table_v,
     ends_v,
     edge_out_v,
-    node_in_v,
-    node_out_v,
     first_v,
     far_hot_v,
     spread_v,
     back_v,
-    new_nodes_v,
-    new_edges_v,
+    node_top_v,
     out_rows,
     in_rows,
     out_sums,
     in_sums,
     load_sem,
-    store_sem,
     sems,
 ):
     node_dev, width = node_v.shape
@@ -102,7 +102,8 @@
                 (edge_in_hbm.at[pl.ds(0, width)], table_v.at[pl.ds(0, width)]),
                 (edge_hbm, edge_v),
                 (edge_out_hbm, edge_out_v),
-                (node_in_hbm, node_in_v),
+                (node_in_hbm.at[pl.ds(0, width)], node_top_v),
+                (node_in_hbm.at[pl.ds(width, width)], node_in_v),
                 (node_out_hbm, node_out_v),
             ]
         )
@@ -208,12 +209,6 @@
     each_peer(lambda peer: arrival(out_rows, in_rows, 0, peer).wait_recv())
     table_v[pl.ds(near, slots), :] = dot(in_rows[...], ends_v[pl.ds(width, width), :]).astype(bf16)
 
-    def store(block):
-        here = pl.ds(pl.multiple_of(block * block_rows, block_rows), block_rows)
-        return pltpu.make_async_copy(
-            new_edges_v.at[here], new_edges_hbm.at[here], store_sem.at[block]
-        )
-
     def after(block, carry):
         here = pl.ds(pl.multiple_of(block * block_rows, block_rows), block_rows)
         first = first_v[here, :] + dot(far_hot_v[here, :], table_v[pl.ds(near, slots), :])
@@ -222,7 +217,6 @@
         updated = residual_norm(old, mixed)
         live = block * block_rows + iota((block_rows, 1), 0) < live_count
         new_edges_v[here, :] = jnp.where(live, updated, old.astype(f32)).astype(bf16)
-        store(block).start()
         return carry
 
     lax.fori_loop(0, blocks, after, 0)
@@ -231,23 +225,40 @@
     each_peer(lambda peer: transfer(out_sums, in_sums, 2, peer).start())
 
     near_sums = dot(spread_v[pl.ds(0, node_dev), :], new_edges_v[...])
-    node_first = dot(node_v[...], node_in_v[pl.ds(0, width), :])
+    node_first_v[...] = dot(node_v[...], node_top_v[...])
     each_peer(lambda peer: arrival(out_sums, in_sums, 2, peer).wait_recv())
-    aggregate = (near_sums + dot(back_v[...], in_sums[...])).astype(bf16)
-    node_first = node_first + dot(aggregate, node_in_v[pl.ds(width, width), :])
+    aggregate_v[...] = (near_sums + dot(back_v[...], in_sums[...])).astype(bf16)
+    each_peer(lambda peer: transfer(out_rows, in_rows, 0, peer).wait_send())
+    each_peer(lambda peer: transfer(out_sums, in_sums, 2, peer).wait_send())
+
+
+def finish_kernel(
+    edges_v,
+    aggregate_v,
+    node_first_v,
+    node_v,
+    node_in_v,
+    node_out_v,
+    new_nodes_hbm,
+    new_edges_hbm,
+    new_nodes_v,
+    sems,
+):
+    stores = []
+    piece = edges_v.shape[0] // store_pieces
+    for number in range(store_pieces):
+        here = pl.ds(number * piece, piece)
+        stores.append(
+            pltpu.make_async_copy(edges_v.at[here], new_edges_hbm.at[here], sems.at[number])
+        )
+        stores[-1].start()
+    node_first = node_first_v[...] + dot(aggregate_v[...], node_in_v[...])
     mixed = dot(half_silu(node_first), node_out_v[...])
     new_nodes_v[...] = residual_norm(node_v[...], mixed).astype(bf16)
-    last = pltpu.make_async_copy(new_nodes_v, new_nodes_hbm, store_sem.at[blocks])
-    last.start()
-    each_peer(lambda peer: transfer(out_rows, in_rows, 0, peer).wait_send())
-    each_peer(lambda peer: transfer(out_sums, in_sums, 2, peer).wait_send())
-
-    def finish(block, carry):
-        store(block).wait()
-        return carry
-
-    lax.fori_loop(0, blocks, finish, 0)
-    last.wait()
+    stores.append(pltpu.make_async_copy(new_nodes_v, new_nodes_hbm, sems.at[store_pieces]))
+    stores[-1].start()
+    for store in stores:
+        store.wait()
 
 
 def shards(
@@ -278,16 +289,19 @@
     blocks = edge_dev // block_rows
     any_space = pl.BlockSpec(memory_space=pl.ANY)
     index_shape = (edge_dev // lanes, lanes)
-    return pl.pallas_call(
+    held = pl.pallas_call(
         functools.partial(kernel, peers, pad),
         out_shape=(
-            jax.ShapeDtypeStruct(node_latent.shape, bf16),
-            jax.ShapeDtypeStruct(edge_latent.shape, bf16),
+            pltpu.VMEM((edge_dev, width), bf16),
+            pltpu.VMEM((node_dev, width), bf16),
+            pltpu.VMEM((node_dev, width), f32),
+            pltpu.VMEM((node_dev, width), bf16),
+            pltpu.VMEM((width, width), bf16),
+            pltpu.VMEM((width, width), bf16),
         ),
         in_specs=[pl.BlockSpec(memory_space=pltpu.SMEM)] + [any_space] * 9,
-        out_specs=(any_space, any_space),
+        out_specs=[pl.BlockSpec(memory_space=pltpu.VMEM)] * 6,
         scratch_shapes=[
-            pltpu.VMEM((node_dev, width), bf16),
             pltpu.VMEM((edge_dev, width), bf16),
             pltpu.VMEM(index_shape, jnp.int32),
             pltpu.VMEM(index_shape, jnp.int32),
@@ -295,24 +309,20 @@
             pltpu.VMEM((width + 2 * node_dev + slots, width), bf16),
             pltpu.VMEM((2 * width, width), bf16),
             pltpu.VMEM((width, width), bf16),
-            pltpu.VMEM((2 * width, width), bf16),
-            pltpu.VMEM((width, width), bf16),
             pltpu.VMEM((edge_dev, width), f32),
             pltpu.VMEM((edge_dev, slots), bf16),
             pltpu.VMEM((node_dev + slots, edge_dev), bf16),
             pltpu.VMEM((node_dev, slots), bf16),
-            pltpu.VMEM((node_dev, width), bf16),
-            pltpu.VMEM((edge_dev, width), bf16),
+            pltpu.VMEM((width, width), bf16),
             pltpu.VMEM((slots, width), bf16),
             pltpu.VMEM((slots, width), bf16),
             pltpu.VMEM((slots, width), bf16),
             pltpu.VMEM((slots, width), bf16),
-            pltpu.SemaphoreType.DMA((10,)),
-            pltpu.SemaphoreType.DMA((blocks + 1,)),
+            pltpu.SemaphoreType.DMA((11,)),
             pltpu.SemaphoreType.DMA((4, peers)),
         ],
         compiler_params=pltpu.CompilerParams(
-            collective_id=0, has_side_effects=True, vmem_limit_bytes=56 * 1024 * 1024
+            collective_id=0, has_side_effects=True, vmem_limit_bytes=58 * 1024 * 1024
         ),
     )(
         edge_count,
@@ -326,6 +336,20 @@
         node_in,
         node_out,
     )
+    return pl.pallas_call(
+        finish_kernel,
+        out_shape=(
+            jax.ShapeDtypeStruct(node_latent.shape, bf16),
+            jax.ShapeDtypeStruct(edge_latent.shape, bf16),
+        ),
+        in_specs=[pl.BlockSpec(memory_space=pltpu.VMEM)] * 6,
+        out_specs=(any_space, any_space),
+        scratch_shapes=[
+            pltpu.VMEM((node_dev, width), bf16),
+            pltpu.SemaphoreType.DMA((store_pieces + 1,)),
+        ],
+        compiler_params=pltpu.CompilerParams(vmem_limit_bytes=40 * 1024 * 1024),
+    )(*held)
 
 
 def solution(mesh):

time: 34.4 us -> 29.8 us (0.87)
  local copies, waits for them, and re-layouts: 4.81 us -> 0 us
    unnamed x2 -> x0, local copies, waits for them, and re-layouts: 4.81 us -> none
    pallas_call x1 -> x2, Pallas kernels: 28.1 us -> 28.3 us  [the longest x1 26.6 us: shards(): pl.pallas_call(functools.partial(kernel, peers, pad), out_shape=(pltpu.VM...]
where the time goes in v2:
time: 29.8 us; the launch traced here: 29.6 us
  Pallas kernels  28.3 us (95%)
  between operations  1.29 us (4%)
    pallas_call x1, Pallas kernels, shards(): pl.pallas_call(functools.partial(kernel, peers, pad), out_shape=(pltpu.VM...  26.6 us
    pallas_call x1, Pallas kernels, shards(): pl.pallas_call(finish_kernel, out_shape=(jax.ShapeDtypeStruct(node_latent...  1.68 us

profile of v2, /device:TPU:0, one launch (start us, length us, event | category | flops | bytes accessed | tf_op | source)
XLA Modules:
  0.0 29.6 jit_solution(1779266001154856842)
XLA Ops:
  1.3 26.6 %shard_map.113 = (bf16[2048,512]{1,0:T(8,128)(2,1)S(1)}, bf16[384,512]{1,0:T(8,128)(2,1)S(1)}, f32[384,512]{1,0:T(8,128)S(1)}, bf16[384,512]{1,0:T(8,128)(2,1)S(...) custom-call(s32[1]{0:T(128)S(6)} %copy.12.count_ref, bf16[384,512]{1,0:T(8,128)(2,1)} %node_hbm.1, ...), custom_call_target="tpu_custom_call" | custom-call | tf_op jit(solution)/shard_map/pallas_call | solution.py:292
  27.9 1.7 %shard_map.114 = (bf16[384,512]{1,0:T(8,128)(2,1)}, bf16[2048,512]{1,0:T(8,128)(2,1)}) custom-call(bf16[2048,512]{1,0:T(8,128)(2,1)S(1)} %get-tuple-element.8.edges_v, bf16[384,512]{1,0:T(8,128)(2,1)S(1)} %get-tuple-element.9.aggregate_v, f32[384,512]{1,0:T(8,128)S(1)} %get-tuple-element.10.node_first_v, bf16[384,512]{1,0:T(8,128)(2,1)S(1)} %get-tuple-element.11.node_v, ...), custom_call_target="tpu_custom_call" | custom-call | tf_op jit(solution)/shard_map/pallas_call | solution.py:339

commit v3 on v2

--- a/solution.py
+++ b/solution.py
@@ -76,7 +76,6 @@
     node_dev, width = node_v.shape
     edge_dev = edge_v.shape[0]
     slots = peers * pad
-    near = width + 2 * node_dev
     blocks = edge_dev // block_rows
     parts = block_rows // lanes
     me = lax.axis_index("space")
@@ -124,7 +123,10 @@
     column = jnp.sum(jnp.where(picked, rows, 0.0), axis=1, keepdims=True)
     wanted = (column.astype(jnp.int32) == iota((slots, node_dev), 1)).astype(f32)
     loads[1].wait()
-    out_rows[...] = dot(wanted.astype(bf16), node_v[...]).astype(bf16)
+    loads[2].wait()
+    received = dot(node_v[...], ends_v[pl.ds(width, width), :]).astype(bf16)
+    table_v[pl.ds(width + node_dev, node_dev), :] = received
+    out_rows[...] = dot(wanted.astype(bf16), received).astype(bf16)
 
     def transfer(source, target, number, peer):
         theirs = pl.ds(pl.multiple_of(peer * pad, pad), pad)
@@ -159,11 +161,7 @@
     each_peer(lambda peer: transfer(out_rows, in_rows, 0, peer).start())
 
     back_v[...] = wanted.T.astype(bf16)
-    loads[2].wait()
     table_v[pl.ds(width, node_dev), :] = dot(node_v[...], ends_v[pl.ds(0, width), :]).astype(bf16)
-    table_v[pl.ds(width + node_dev, node_dev), :] = dot(
-        node_v[...], ends_v[pl.ds(width, width), :]
-    ).astype(bf16)
     for load in loads[3:]:
         load.wait()
     live_count = count_ref[0]
@@ -192,7 +190,7 @@
         left = jnp.concatenate(
             [edge_v[here, :], hot(senders, 0, node_dev), hot(receivers, 0, node_dev)], axis=1
         )
-        first_v[here, :] = dot(left, table_v[pl.ds(0, near), :])
+        first_v[here, :] = dot(left, table_v[...])
         far_hot_v[here, :] = hot(receivers, node_dev, node_dev + slots)
         for j in range(parts):
             place = block * block_rows + j * lanes
@@ -207,11 +205,10 @@
     lax.fori_loop(0, blocks, before, 0)
 
     each_peer(lambda peer: arrival(out_rows, in_rows, 0, peer).wait_recv())
-    table_v[pl.ds(near, slots), :] = dot(in_rows[...], ends_v[pl.ds(width, width), :]).astype(bf16)
 
     def after(block, carry):
         here = pl.ds(pl.multiple_of(block * block_rows, block_rows), block_rows)
-        first = first_v[here, :] + dot(far_hot_v[here, :], table_v[pl.ds(near, slots), :])
+        first = first_v[here, :] + dot(far_hot_v[here, :], in_rows[...])
         mixed = dot(half_silu(first), edge_out_v[...])
         old = edge_v[here, :]
         updated = residual_norm(old, mixed)
@@ -219,17 +216,17 @@
         new_edges_v[here, :] = jnp.where(live, updated, old.astype(f32)).astype(bf16)
         return carry
 
-    lax.fori_loop(0, blocks, after, 0)
+    lax.fori_loop(0, blocks, after, 0, unroll=True)
 
     out_sums[...] = dot(spread_v[pl.ds(node_dev, slots), :], new_edges_v[...]).astype(bf16)
     each_peer(lambda peer: transfer(out_sums, in_sums, 2, peer).start())
 
     near_sums = dot(spread_v[pl.ds(0, node_dev), :], new_edges_v[...])
     node_first_v[...] = dot(node_v[...], node_top_v[...])
+    each_peer(lambda peer: transfer(out_rows, in_rows, 0, peer).wait_send())
+    each_peer(lambda peer: transfer(out_sums, in_sums, 2, peer).wait_send())
     each_peer(lambda peer: arrival(out_sums, in_sums, 2, peer).wait_recv())
     aggregate_v[...] = (near_sums + dot(back_v[...], in_sums[...])).astype(bf16)
-    each_peer(lambda peer: transfer(out_rows, in_rows, 0, peer).wait_send())
-    each_peer(lambda peer: transfer(out_sums, in_sums, 2, peer).wait_send())
 
 
 def finish_kernel(
@@ -306,7 +303,7 @@
             pltpu.VMEM(index_shape, jnp.int32),
             pltpu.VMEM(index_shape, jnp.int32),
             pltpu.VMEM((peers, pad), jnp.int32),
-            pltpu.VMEM((width + 2 * node_dev + slots, width), bf16),
+            pltpu.VMEM((width + 2 * node_dev, width), bf16),
             pltpu.VMEM((2 * width, width), bf16),
             pltpu.VMEM((width, width), bf16),
             pltpu.VMEM((edge_dev, width), f32),

time: 29.8 us -> 27 us (0.906)
  Pallas kernels: 28.3 us -> 25.4 us
    pallas_call x1, Pallas kernels: 26.6 us -> 23.7 us  [shards(): pl.pallas_call(functools.partial(kernel, peers, pad), out_shape=(pltpu.VM...]
where the time goes in v3:
time: 27 us; the launch traced here: 26.7 us
  Pallas kernels  25.4 us (94%)
  between operations  1.29 us (5%)
    pallas_call x1, Pallas kernels, shards(): pl.pallas_call(functools.partial(kernel, peers, pad), out_shape=(pltpu.VM...  23.7 us
    pallas_call x1, Pallas kernels, shards(): pl.pallas_call(finish_kernel, out_shape=(jax.ShapeDtypeStruct(node_latent...  1.68 us

profile of v3, /device:TPU:0, one launch (start us, length us, event | category | flops | bytes accessed | tf_op | source)
XLA Modules:
  0.0 26.7 jit_solution(981961533456415671)
XLA Ops:
  1.3 23.7 %shard_map.113 = (bf16[2048,512]{1,0:T(8,128)(2,1)S(1)}, bf16[384,512]{1,0:T(8,128)(2,1)S(1)}, f32[384,512]{1,0:T(8,128)S(1)}, bf16[384,512]{1,0:T(8,128)(2,1)S(...) custom-call(s32[1]{0:T(128)S(6)} %copy.12.count_ref, bf16[384,512]{1,0:T(8,128)(2,1)} %node_hbm.1, ...), custom_call_target="tpu_custom_call" | custom-call | tf_op jit(solution)/shard_map/pallas_call | solution.py:289
  25.0 1.7 %shard_map.114 = (bf16[384,512]{1,0:T(8,128)(2,1)}, bf16[2048,512]{1,0:T(8,128)(2,1)}) custom-call(bf16[2048,512]{1,0:T(8,128)(2,1)S(1)} %get-tuple-element.8.edges_v, bf16[384,512]{1,0:T(8,128)(2,1)S(1)} %get-tuple-element.9.aggregate_v, f32[384,512]{1,0:T(8,128)S(1)} %get-tuple-element.10.node_first_v, bf16[384,512]{1,0:T(8,128)(2,1)S(1)} %get-tuple-element.11.node_v, ...), custom_call_target="tpu_custom_call" | custom-call | tf_op jit(solution)/shard_map/pallas_call | solution.py:336

commit v4 on v3

--- a/solution.py
+++ b/solution.py
@@ -202,23 +202,23 @@
             )
         return carry
 
-    lax.fori_loop(0, blocks, before, 0)
+    lax.fori_loop(0, blocks, before, 0, unroll=2)
 
     each_peer(lambda peer: arrival(out_rows, in_rows, 0, peer).wait_recv())
 
-    def after(block, carry):
+    def after(block, sums):
         here = pl.ds(pl.multiple_of(block * block_rows, block_rows), block_rows)
         first = first_v[here, :] + dot(far_hot_v[here, :], in_rows[...])
         mixed = dot(half_silu(first), edge_out_v[...])
         old = edge_v[here, :]
         updated = residual_norm(old, mixed)
         live = block * block_rows + iota((block_rows, 1), 0) < live_count
-        new_edges_v[here, :] = jnp.where(live, updated, old.astype(f32)).astype(bf16)
-        return carry
-
-    lax.fori_loop(0, blocks, after, 0, unroll=True)
-
-    out_sums[...] = dot(spread_v[pl.ds(node_dev, slots), :], new_edges_v[...]).astype(bf16)
+        kept = jnp.where(live, updated, old.astype(f32)).astype(bf16)
+        new_edges_v[here, :] = kept
+        return sums + dot(spread_v[pl.ds(node_dev, slots), here], kept)
+
+    far_sums = lax.fori_loop(0, blocks, after, jnp.zeros((slots, width), f32), unroll=True)
+    out_sums[...] = far_sums.astype(bf16)
     each_peer(lambda peer: transfer(out_sums, in_sums, 2, peer).start())
 
     near_sums = dot(spread_v[pl.ds(0, node_dev), :], new_edges_v[...])

time: 27 us -> 28.9 us (1.070)
  Pallas kernels: 25.4 us -> 27.4 us
    pallas_call x1, Pallas kernels: 23.7 us -> 25.7 us  [shards(): pl.pallas_call(functools.partial(kernel, peers, pad), out_shape=(pltpu.VM...]
where the time goes in v4:
time: 28.9 us; the launch traced here: 28.7 us
  Pallas kernels  27.4 us (95%)
  between operations  1.29 us (4%)
    pallas_call x1, Pallas kernels, shards(): pl.pallas_call(functools.partial(kernel, peers, pad), out_shape=(pltpu.VM...  25.7 us
    pallas_call x1, Pallas kernels, shards(): pl.pallas_call(finish_kernel, out_shape=(jax.ShapeDtypeStruct(node_latent...  1.68 us

profile of v4, /device:TPU:0, one launch (start us, length us, event | category | flops | bytes accessed | tf_op | source)
XLA Modules:
  0.0 28.7 jit_solution(6459960372894397764)
XLA Ops:
  1.3 25.7 %shard_map.113 = (bf16[2048,512]{1,0:T(8,128)(2,1)S(1)}, bf16[384,512]{1,0:T(8,128)(2,1)S(1)}, f32[384,512]{1,0:T(8,128)S(1)}, bf16[384,512]{1,0:T(8,128)(2,1)S(...) custom-call(s32[1]{0:T(128)S(6)} %copy.12.count_ref, bf16[384,512]{1,0:T(8,128)(2,1)} %node_hbm.1, ...), custom_call_target="tpu_custom_call" | custom-call | tf_op jit(solution)/shard_map/pallas_call | solution.py:289
  27.0 1.7 %shard_map.114 = (bf16[384,512]{1,0:T(8,128)(2,1)}, bf16[2048,512]{1,0:T(8,128)(2,1)}) custom-call(bf16[2048,512]{1,0:T(8,128)(2,1)S(1)} %get-tuple-element.8.edges_v, bf16[384,512]{1,0:T(8,128)(2,1)S(1)} %get-tuple-element.9.aggregate_v, f32[384,512]{1,0:T(8,128)S(1)} %get-tuple-element.10.node_first_v, bf16[384,512]{1,0:T(8,128)(2,1)S(1)} %get-tuple-element.11.node_v, ...), custom_call_target="tpu_custom_call" | custom-call | tf_op jit(solution)/shard_map/pallas_call | solution.py:336
